TPU v7x, 32 devices: a whole 2x2x4 slice. The times are simulated.
32 devices in a mesh: shell: 2 (over y), row: 4 (over x, core), col: 4 (over z).
Axes of the slice: x: 2, y: 2, z: 4, core: 2. Of those that a mesh axis runs over, the one named last changes fastest.
Arguments:
- left_basis: bfloat16 [2, 1024, 1536], P(None, 'row', 'shell'), may hold values from -6 to 6
- right_basis: bfloat16 [2, 1536, 2048], P(None, 'shell', 'col'), may hold values from -0.15625 to 0.15625
- point_weight: float32 [1536], P('shell'), may hold values from 0.3 to 3
- shell_index: int32 [1536], P('shell'), may hold values from 0 to 11
- green_table: float32 [12, 2], replicated, may hold values from -4 to 4
- pivot_rows: int32 [512], replicated, may hold values from 0 to 1023, as said below
- diag_inverse: bfloat16 [2, 512, 512], replicated, may hold values from -0.005859375 to 0.005859375
Outputs:
- factored: float32 [2, 4, 2, 128, 2048], P(None, 'row', 'shell', None, 'col')
Inputs may be any that keep to these rules, and one draw needn't show every extreme that they name: `pivot_rows`: 512 distinct matrix rows.
All inputs are finite; a program needn't handle non-finite values.
Results may differ from a plain program's by a relative error of at most 0.0056.
Values may be sent and summed in bfloat16 or wider, within the bound.
A program may use at most 128 MiB of HBM per device.

v0:
```python
import functools
import math
import jax
import jax.numpy as jnp
from jax import lax
from jax.experimental import pallas as pl
from jax.experimental.pallas import tpu as pltpu
from jax.sharding import PartitionSpec as P

MESH = pl.DeviceIdType.MESH
CORES = 2


def kernel(shells, rows, cols, chunk, left_hbm, right_hbm, point_hbm, shell_hbm, green_hbm, pivot_hbm,
           inverse_hbm, out_ref, left_ref, right_ref, inverse_ref, point_ref, shell_ref, green_ref, pivot_ref, weights, weighted, product, part,
           outgoing, incoming, coupling, owned, mult, select, spread, in_sem, y_send, y_recv, x_send,
           x_recv, f_send, f_recv, m_send, m_recv):
    s = lax.axis_index("shell")
    r = lax.axis_index("row")
    col = lax.axis_index("col")
    chips = rows // CORES
    h = r // CORES
    core = lax.rem(r, CORES)
    sibling = h * CORES + (CORES - 1 - core)
    points = right_ref.shape[1]
    width = right_ref.shape[2]
    tile_rows = left_ref.shape[1]
    own = tile_rows // shells
    pieces = own // chunk
    half = mult.shape[2]
    batch = chunk
    halves = batch // half
    bf16, f32 = jnp.bfloat16, jnp.float32

    slab = 256
    slabs = points // slab
    right_in = [
        pltpu.make_async_copy(
            right_hbm.at[:, pl.ds(b * slab, slab)], right_ref.at[:, pl.ds(b * slab, slab)], in_sem.at[b]
        )
        for b in range(slabs)
    ]
    left_in = pltpu.make_async_copy(left_hbm, left_ref, in_sem.at[slabs])
    inverse_in = pltpu.make_async_copy(inverse_hbm, inverse_ref, in_sem.at[slabs + 1])
    small_in = [
        pltpu.make_async_copy(source, target, in_sem.at[slabs + 2 + i])
        for i, (source, target) in enumerate([
            (point_hbm, point_ref), (shell_hbm, shell_ref), (green_hbm, green_ref), (pivot_hbm, pivot_ref)
        ])
    ]
    for copy in small_in[:3]:
        copy.start()
    right_in[0].start()
    left_in.start()
    for copy in right_in[1:]:
        copy.start()
    small_in[3].start()

    @pl.when(col == 0)
    def _():
        inverse_in.start()

    barrier = pltpu.get_barrier_semaphore()

    def greet(**where):
        pl.semaphore_signal(barrier, inc=1, device_id=where, device_id_type=MESH)

    for o in range(1, shells):
        greet(shell=lax.rem(s + o, shells))
    for d in range(1, chips):
        greet(row=lax.rem(h + d, chips) * CORES + core)
    greet(row=sibling)

    @pl.when(col > 0)
    def _():
        greet(col=col - 1)

    @pl.when(col < cols - 1)
    def _():
        greet(col=col + 1)

    for copy in small_in[:3]:
        copy.wait()
    count = green_ref.shape[1]
    padded = -(-count // 16) * 16
    index = shell_ref[...].reshape(1, points)
    match = lax.broadcasted_iota(jnp.int32, (padded, points), 0) == index

    def pieces_of(value):
        first = value.astype(bf16).astype(f32)
        second = (value - first).astype(bf16).astype(f32)
        return first, second, value - first - second

    hot = [jnp.where(match, piece, 0.0).astype(bf16) for piece in pieces_of(point_ref[...].reshape(1, points))]
    square = (padded, count)
    same = lax.broadcasted_iota(jnp.int32, square, 0) == lax.broadcasted_iota(jnp.int32, square, 1)
    table = jnp.concatenate(
        [
            jnp.broadcast_to(
                jnp.sum(
                    jnp.where(same, jnp.broadcast_to(green_ref[i : i + 1, :], square), 0.0),
                    axis=1, keepdims=True,
                ),
                (padded, 128),
            )
            for i in range(2)
        ],
        axis=1,
    )
    green = [piece.astype(bf16) for piece in pieces_of(table)]
    pairs = [(i, j) for i in range(3) for j in range(3 - i)]
    weights[...] = lax.dot_general(
        jnp.concatenate([hot[i] for i, _ in pairs], axis=0),
        jnp.concatenate([green[j] for _, j in pairs], axis=0),
        (((0,), (0,)), ((), ())),
        preferred_element_type=f32,
    )

    def span(first, size):
        return pl.ds(pl.multiple_of(first, size), size)

    def y_copy(o, j, c, group):
        at = span(group * own + c * chunk, chunk)
        return pltpu.make_async_remote_copy(
            src_ref=outgoing.at[at], dst_ref=incoming.at[o - 1, at],
            send_sem=y_send.at[o - 1, j, c], recv_sem=y_recv.at[o - 1, j, c],
            device_id={"shell": lax.rem(s + o, shells)}, device_id_type=MESH,
        )

    def x_copy(d, j, c, group, row):
        at = span(row * tile_rows + group * own + c * chunk, chunk)
        return pltpu.make_async_remote_copy(
            src_ref=coupling.at[at], dst_ref=coupling.at[at],
            send_sem=x_send.at[d - 1, j, c], recv_sem=x_recv.at[d - 1, j, c],
            device_id={"row": lax.rem(h + d, chips) * CORES + core}, device_id_type=MESH,
        )

    def f_copy(d, j, c, group, row):
        at = span(row * tile_rows + group * own + c * chunk, chunk)
        return pltpu.make_async_remote_copy(
            src_ref=coupling.at[at], dst_ref=coupling.at[at],
            send_sem=f_send.at[d, j, c], recv_sem=f_recv.at[d, j, c],
            device_id={"row": sibling}, device_id_type=MESH,
        )

    def m_copy(i):
        return pltpu.make_async_remote_copy(
            src_ref=mult.at[i], dst_ref=mult.at[i], send_sem=m_send.at[i], recv_sem=m_recv.at[i],
            device_id={"col": col + 1}, device_id_type=MESH,
        )

    def left_rows(group, at):
        rows_at = span(group * own, own)
        return jnp.concatenate([left_ref[0, rows_at, at], left_ref[1, rows_at, at]], axis=0)

    def combine(first_row, size):
        top = product[first_row : first_row + size, :]
        low = product[own + first_row : own + first_row + size, :]
        return top[:, :width] - low[:, width:], top[:, width:] + low[:, :width]

    first = lax.rem(s + 1, shells)
    for b in range(slabs):
        at = pl.ds(b * slab, slab)
        right_in[b].wait()
        w_real = jnp.concatenate([weights[at, :128]] * (width // 128), axis=1)
        w_imag = jnp.concatenate([weights[at, 128:]] * (width // 128), axis=1)
        b_real = right_ref[0, at, :].astype(f32)
        b_imag = right_ref[1, at, :].astype(f32)
        weighted[at, :width] = (w_real * b_real - w_imag * b_imag).astype(bf16)
        weighted[at, width:] = (w_real * b_imag + w_imag * b_real).astype(bf16)
        if b == 0:
            left_in.wait()
        term = jnp.dot(left_rows(first, at), weighted[at, :], preferred_element_type=f32)
        product[...] = term if b == 0 else product[...] + term

    for k in range(shells):
        group = lax.rem(s + 1 + k, shells)
        if k > 0:
            product[...] = jnp.dot(
                left_rows(group, pl.ds(0, points)), weighted[...], preferred_element_type=f32
            )
        if k == 0:
            line = jnp.minimum(col, 1) + jnp.minimum(cols - 1 - col, 1)
            pl.semaphore_wait(barrier, shells - 1 + chips + line)
        for c in range(pieces):
            at = span(group * own + c * chunk, chunk)
            real, imag = combine(c * chunk, chunk)
            part[at, :width] = real
            part[at, width:] = imag
            outgoing[at, :width] = real.astype(bf16)
            outgoing[at, width:] = imag.astype(bf16)
            for o in range(1, shells):
                y_copy(o, (1 + k - o) % shells, c, group).start()

    def choose(i):
        pivots = pivot_ref[...].reshape(1, -1)
        line = lax.broadcasted_iota(jnp.int32, (128, pivots.shape[1]), 0) + i * 128
        select[i * 128 : (i + 1) * 128, :] = jnp.where(line == pivots, 1.0, 0.0).astype(bf16)

    def take_y(j, c):
        group = lax.rem(s + j, shells)
        at = span(group * own + c * chunk, chunk)
        total = part[at, :]
        for o in range(1, shells):
            y_copy(o, j, c, group).wait_recv()
            total = total + incoming[o - 1, at, :].astype(f32)
        coupling[span(r * tile_rows + group * own + c * chunk, chunk), :] = total.astype(bf16)
        if j == 0:
            owned[c * chunk : (c + 1) * chunk, :] = total
        for d in range(1, chips):
            x_copy(d, j, c, group, r).start()
        f_copy(0, j, c, group, r).start()
        if j == 0 and (c + 1) * chunk % batch == 0:

            @pl.when(col == 0)
            def _():
                base = (c + 1) * chunk - batch
                if base == 0:
                    inverse_in.wait()
                panel = owned[base : base + batch, :]
                high = panel.astype(bf16)
                low = (panel - high.astype(f32)).astype(bf16)
                four = jnp.concatenate(
                    [high[:, :width], low[:, :width], high[:, width:], low[:, width:]], axis=0
                )
                by_real = jnp.dot(four, inverse_ref[0], preferred_element_type=f32)
                by_imag = jnp.dot(four, inverse_ref[1], preferred_element_type=f32)

                def pick(value, at):
                    return value[at : at + batch] + value[at + batch : at + 2 * batch]

                m_real = (pick(by_real, 0) - pick(by_imag, 2 * batch)).astype(bf16)
                m_imag = (pick(by_imag, 0) + pick(by_real, 2 * batch)).astype(bf16)
                for p in range(halves):
                    i = base // half + p
                    mult[i, 0] = m_real[p * half : (p + 1) * half]
                    mult[i, 1] = m_imag[p * half : (p + 1) * half]
                    if cols > 1:
                        m_copy(i).start()

    def take_x(j, c):
        group = lax.rem(s + j, shells)
        for d in range(1, chips):
            row = lax.rem(h - d + chips, chips) * CORES + core
            x_copy(d, j, c, group, row).wait_recv()
            f_copy(d, j, c, group, row).start()

    passes = own // half

    def pass_mult(turn):
        for i in range(passes):
            k, odd = divmod(turn - i, 2)
            if odd == 0 and 0 < k < cols - 1:

                @pl.when(col == k)
                def _():
                    m_copy(i).wait_recv()
                    m_copy(i).start()

    def take_sibling(d, j, c):
        group = lax.rem(s + j, shells)
        row = lax.rem(h - d + chips, chips) * CORES + (CORES - 1 - core)
        f_copy(d, j, c, group, row).wait_recv()

    steps = [(j, c) for j in range(shells) for c in range(pieces)]
    lag = 2
    slices = select.shape[0] // 128
    small_in[3].wait()
    for n, (j, c) in enumerate(steps):
        take_y(j, c)
        pass_mult(n)
        if n >= lag:
            take_x(*steps[n - lag])
        for i in range(n * slices // len(steps), (n + 1) * slices // len(steps)):
            choose(i)

    for turn in range(len(steps), passes + 2 * cols):
        pass_mult(turn)

    @pl.when((col == cols - 1) & (col > 0))
    def _():
        for i in range(passes):
            m_copy(i).wait_recv()

    factors = jnp.concatenate([mult[i, p] for p in range(2) for i in range(passes)], axis=0)
    spread[...] = lax.dot_general(
        factors, select[...], (((1,), (1,)), ((), ())), preferred_element_type=f32
    ).astype(bf16)
    for j, c in steps:
        take_sibling(0, j, c)
    near = span(h * CORES * tile_rows, CORES * tile_rows)
    product[...] = jnp.dot(spread[:, near], coupling[near, :], preferred_element_type=f32)
    for j in range(shells):
        if j == shells - 1:
            for step in steps[-lag:]:
                take_x(*step)
        group = lax.rem(s + j, shells)
        for d in range(1, chips):
            for c in range(pieces):
                take_sibling(d, j, c)
            first_row = lax.rem(h - d + chips, chips) * CORES * tile_rows + group * own
            spots = [span(first_row + i * tile_rows, own) for i in range(CORES)]
            product[...] += jnp.dot(
                jnp.concatenate([spread[:, at] for at in spots], axis=1),
                jnp.concatenate([coupling[at, :] for at in spots], axis=0),
                preferred_element_type=f32,
            )
    real, imag = combine(0, own)
    out_ref[0, 0, 0] = owned[:, :width] - real
    out_ref[1, 0, 0] = owned[:, width:] - imag

    for j, c in steps:
        group = lax.rem(s + j, shells)
        for o in range(1, shells):
            y_copy(o, j, c, group).wait_send()
        f_copy(0, j, c, group, r).wait_send()
        for d in range(1, chips):
            x_copy(d, j, c, group, r).wait_send()
            f_copy(d, j, c, group, lax.rem(h - d + chips, chips) * CORES + core).wait_send()

    @pl.when(col < cols - 1)
    def _():
        for i in range(passes):
            m_copy(i).wait_send()


def body(sizes, left_basis, right_basis, point_weight, shell_index, green_table, pivot_rows, diag_inverse):
    shells, rows, cols = sizes
    chips = rows // CORES
    tile_rows, points = left_basis.shape[1:]
    width = right_basis.shape[2]
    own = tile_rows // shells
    chunk = own // 4
    half = chunk
    pieces = own // chunk
    all_rows = rows * tile_rows
    bf16, f32 = jnp.bfloat16, jnp.float32
    vmem = pl.BlockSpec(memory_space=pltpu.VMEM)
    sems = pltpu.SemaphoreType.DMA
    buffers = [
        ((2, tile_rows, points), bf16),
        ((2, points, width), bf16),
        (diag_inverse.shape, bf16),
        (point_weight.shape, f32),
        (shell_index.shape, jnp.int32),
        (green_table.shape[::-1], f32),
        (pivot_rows.shape, jnp.int32),
        ((points, 256), f32),
        ((points, 2 * width), bf16),
        ((2 * own, 2 * width), f32),
        ((tile_rows, 2 * width), f32),
        ((tile_rows, 2 * width), bf16),
        ((max(shells - 1, 1), tile_rows, 2 * width), bf16),
        ((all_rows, 2 * width), bf16),
        ((own, 2 * width), f32),
        ((own // half, 2, half, width), bf16),
        ((all_rows, pivot_rows.shape[0]), bf16),
        ((2 * own, all_rows), bf16),
    ]
    held = sum(math.prod(shape) * jnp.dtype(kind).itemsize for shape, kind in buffers)
    return pl.pallas_call(
        functools.partial(kernel, shells, rows, cols, chunk),
        out_shape=pltpu.VMEM((2, 1, 1, own, width), f32),
        in_specs=[pl.BlockSpec(memory_space=pltpu.HBM)] * 7,
        out_specs=vmem,
        scratch_shapes=[pltpu.VMEM(shape, kind) for shape, kind in buffers] + [
            sems((points // 256 + 6,)),
            sems((max(shells - 1, 1), shells, pieces)),
            sems((max(shells - 1, 1), shells, pieces)),
            sems((max(chips - 1, 1), shells, pieces)),
            sems((max(chips - 1, 1), shells, pieces)),
            sems((chips, shells, pieces)),
            sems((chips, shells, pieces)),
            sems((own // half,)),
            sems((own // half,)),
        ],
        compiler_params=pltpu.CompilerParams(
            collective_id=0, has_side_effects=True, vmem_limit_bytes=56 * 2**20
        ),
        cost_estimate=pl.CostEstimate(
            flops=2 * tile_rows * 2 * points * 2 * width + 4 * own * all_rows * 2 * width,
            bytes_accessed=8 * 2**20,
            transcendentals=0,
        ),
    )(left_basis, right_basis, point_weight, shell_index, green_table.T, pivot_rows, diag_inverse)


def solution(mesh):
    sizes = tuple(mesh.shape[name] for name in ("shell", "row", "col"))
    return jax.shard_map(
        functools.partial(body, sizes),
        mesh=mesh,
        in_specs=(
            P(None, "row", "shell"),
            P(None, "shell", "col"),
            P("shell"),
            P("shell"),
            P(),
            P(),
            P(),
        ),
        out_specs=P(None, "row", "shell", None, "col"),
        check_vma=False,
    )
```

profile of v0, /device:TPU:1, one launch (start us, length us, event | category | flops | bytes accessed | tf_op | source)
XLA Modules:
  0.0 23.7 jit_solution(935453339765935867)
XLA Ops:
  0.0 22.9 %shard_map.73 = f32[2,1,1,128,512]{4,3,2,1,0:T(8,128)S(1)} custom-call(bf16[2,256,768]{2,1,0:T(8,128)(2,1)} %left_hbm.1, bf16[2,768,512]{2,1,0:T(8,128)(2,1)} %right_hbm.1, f32[768]{0:T(1024)} %point_hbm.1, s32[768]{0:T(1024)} %shell_hbm.1, f32[2,12]{1,0:T(2,128)} %bitcast.1, s32[512]{0:T(512)} %pivot_hbm.1, bf16[2,512,512]{2,1,0:T(8,128)(2,1)} %inverse_hbm.1), custom_call_target="tpu_custom_call" | custom-call | flops 1342177280 | bytes 8388608 | tf_op jit(solution)/shard_map/pallas_call | solution.py:361
  22.9 0.8 %copy.9 = f32[2,1,1,128,512]{4,3,2,1,0:T(8,128)} copy(f32[2,1,1,128,512]{4,3,2,1,0:T(8,128)S(1)} %shard_map.73) | data formatting | bytes 1048576
where the time goes:
time: 23.9 us; the launch traced here: 23.7 us
  Pallas kernels  22.9 us (96%)
  local copies, waits for them, and re-layouts  0.8 us (3%)
    pallas_call x1, Pallas kernels, body(): pl.pallas_call(functools.partial(kernel, shells, rows, cols, chunk), out_...  22.9 us
    unnamed x1, local copies, waits for them, and re-layouts  0.8 us

commit v1 on v0

--- a/solution.py
+++ b/solution.py
@@ -29,6 +29,7 @@
     pieces = own // chunk
     half = mult.shape[2]
     batch = chunk
+    lanes = 128
     halves = batch // half
     bf16, f32 = jnp.bfloat16, jnp.float32
 
@@ -159,25 +160,38 @@
         return top[:, :width] - low[:, width:], top[:, width:] + low[:, :width]
 
     first = lax.rem(s + 1, shells)
-    for b in range(slabs):
-        at = pl.ds(b * slab, slab)
-        right_in[b].wait()
-        w_real = jnp.concatenate([weights[at, :128]] * (width // 128), axis=1)
-        w_imag = jnp.concatenate([weights[at, 128:]] * (width // 128), axis=1)
-        b_real = right_ref[0, at, :].astype(f32)
-        b_imag = right_ref[1, at, :].astype(f32)
-        weighted[at, :width] = (w_real * b_real - w_imag * b_imag).astype(bf16)
-        weighted[at, width:] = (w_real * b_imag + w_imag * b_real).astype(bf16)
-        if b == 0:
-            left_in.wait()
-        term = jnp.dot(left_rows(first, at), weighted[at, :], preferred_element_type=f32)
-        product[...] = term if b == 0 else product[...] + term
+    every = pl.ds(0, points)
+    for copy in right_in:
+        copy.wait()
+    left_in.wait()
+
+    def pair(b):
+        return pl.ds(b * lanes, lanes), pl.ds(width + b * lanes, lanes)
+
+    for b in range(width // lanes):
+        re, im = pair(b)
+        w_real = weights[:, :lanes]
+        w_imag = weights[:, lanes:]
+        b_real = right_ref[0, :, re].astype(f32)
+        b_imag = right_ref[1, :, re].astype(f32)
+        both = jnp.concatenate(
+            [
+                (w_real * b_real - w_imag * b_imag).astype(bf16),
+                (w_real * b_imag + w_imag * b_real).astype(bf16),
+            ],
+            axis=1,
+        )
+        weighted[:, re] = both[:, :lanes]
+        weighted[:, im] = both[:, lanes:]
+        term = jnp.dot(left_rows(first, every), both, preferred_element_type=f32)
+        product[:, re] = term[:, :lanes]
+        product[:, im] = term[:, lanes:]
 
     for k in range(shells):
         group = lax.rem(s + 1 + k, shells)
         if k > 0:
             product[...] = jnp.dot(
-                left_rows(group, pl.ds(0, points)), weighted[...], preferred_element_type=f32
+                left_rows(group, every), weighted[...], preferred_element_type=f32
             )
         if k == 0:
             line = jnp.minimum(col, 1) + jnp.minimum(cols - 1 - col, 1)
@@ -277,6 +291,9 @@
     for turn in range(len(steps), passes + 2 * cols):
         pass_mult(turn)
 
+    for step in steps[-lag:-1]:
+        take_x(*step)
+
     @pl.when((col == cols - 1) & (col > 0))
     def _():
         for i in range(passes):
@@ -290,24 +307,34 @@
         take_sibling(0, j, c)
     near = span(h * CORES * tile_rows, CORES * tile_rows)
     product[...] = jnp.dot(spread[:, near], coupling[near, :], preferred_element_type=f32)
-    for j in range(shells):
-        if j == shells - 1:
-            for step in steps[-lag:]:
-                take_x(*step)
+    take_x(*steps[-1])
+
+    def far_spots(j, d):
         group = lax.rem(s + j, shells)
+        for c in range(pieces):
+            take_sibling(d, j, c)
+        first_row = lax.rem(h - d + chips, chips) * CORES * tile_rows + group * own
+        return [span(first_row + i * tile_rows, own) for i in range(CORES)]
+
+    def far_product(spots, re, im):
+        return jnp.dot(
+            jnp.concatenate([spread[:, at] for at in spots], axis=1),
+            jnp.concatenate(
+                [jnp.concatenate([coupling[at, re], coupling[at, im]], axis=1) for at in spots], axis=0
+            ),
+            preferred_element_type=f32,
+        )
+
+    for j in range(shells - 1):
         for d in range(1, chips):
-            for c in range(pieces):
-                take_sibling(d, j, c)
-            first_row = lax.rem(h - d + chips, chips) * CORES * tile_rows + group * own
-            spots = [span(first_row + i * tile_rows, own) for i in range(CORES)]
-            product[...] += jnp.dot(
-                jnp.concatenate([spread[:, at] for at in spots], axis=1),
-                jnp.concatenate([coupling[at, :] for at in spots], axis=0),
-                preferred_element_type=f32,
-            )
-    real, imag = combine(0, own)
-    out_ref[0, 0, 0] = owned[:, :width] - real
-    out_ref[1, 0, 0] = owned[:, width:] - imag
+            spots = far_spots(j, d)
+            product[...] += far_product(spots, pl.ds(0, width), pl.ds(width, width))
+    last = [at for d in range(1, chips) for at in far_spots(shells - 1, d)]
+    for b in range(width // lanes):
+        re, im = pair(b)
+        four = jnp.concatenate([product[:, re], product[:, im]], axis=1) + far_product(last, re, im)
+        out_ref[0, 0, 0, :, re] = owned[:, re] - (four[:own, :lanes] - four[own:, lanes:])
+        out_ref[1, 0, 0, :, re] = owned[:, im] - (four[:own, lanes:] + four[own:, :lanes])
 
     for j, c in steps:
         group = lax.rem(s + j, shells)

time: 23.9 us -> 24.3 us (1.017)
  Pallas kernels: 22.9 us -> 23.3 us
    pallas_call x1, Pallas kernels: 22.9 us -> 23.3 us  [body(): pl.pallas_call(functools.partial(kernel, shells, rows, cols, chunk), out_...]
where the time goes in v1:
time: 24.3 us; the launch traced here: 24.1 us
  Pallas kernels  23.3 us (96%)
  local copies, waits for them, and re-layouts  0.8 us (3%)
    pallas_call x1, Pallas kernels, body(): pl.pallas_call(functools.partial(kernel, shells, rows, cols, chunk), out_...  23.3 us
    unnamed x1, local copies, waits for them, and re-layouts  0.8 us

profile of v1, /device:TPU:1, one launch (start us, length us, event | category | flops | bytes accessed | tf_op | source)
XLA Modules:
  0.0 24.1 jit_solution(15479814104290545537)
XLA Ops:
  0.0 23.3 %shard_map.73 = f32[2,1,1,128,512]{4,3,2,1,0:T(8,128)S(1)} custom-call(bf16[2,256,768]{2,1,0:T(8,128)(2,1)} %left_hbm.1, bf16[2,768,512]{2,1,0:T(8,128)(2,1)} %right_hbm.1, f32[768]{0:T(1024)} %point_hbm.1, s32[768]{0:T(1024)} %shell_hbm.1, f32[2,12]{1,0:T(2,128)} %bitcast.1, s32[512]{0:T(512)} %pivot_hbm.1, bf16[2,512,512]{2,1,0:T(8,128)(2,1)} %inverse_hbm.1), custom_call_target="tpu_custom_call" | custom-call | flops 1342177280 | bytes 8388608 | tf_op jit(solution)/shard_map/pallas_call | solution.py:388
  23.3 0.8 %copy.9 = f32[2,1,1,128,512]{4,3,2,1,0:T(8,128)} copy(f32[2,1,1,128,512]{4,3,2,1,0:T(8,128)S(1)} %shard_map.73) | data formatting | bytes 1048576

commit v2 on v0

--- a/solution.py
+++ b/solution.py
@@ -28,8 +28,16 @@
     own = tile_rows // shells
     pieces = own // chunk
     half = mult.shape[2]
-    batch = chunk
-    halves = batch // half
+
+    def places(sizes):
+        return [(c, sum(sizes[:c]), size) for c, size in enumerate(sizes)]
+
+    def parts(j):
+        return places([chunk] * pieces)
+
+    def bundles(j):
+        return places([own - 2 * chunk, chunk, chunk] if j == shells - 1 else [own])
+
     bf16, f32 = jnp.bfloat16, jnp.float32
 
     slab = 256
@@ -117,26 +125,29 @@
     )
 
     def span(first, size):
-        return pl.ds(pl.multiple_of(first, size), size)
-
-    def y_copy(o, j, c, group):
-        at = span(group * own + c * chunk, chunk)
+        return pl.ds(pl.multiple_of(first, math.gcd(size, chunk)), size)
+
+    def y_copy(o, j, piece, group):
+        c, start, size = piece
+        at = span(group * own + start, size)
         return pltpu.make_async_remote_copy(
             src_ref=outgoing.at[at], dst_ref=incoming.at[o - 1, at],
             send_sem=y_send.at[o - 1, j, c], recv_sem=y_recv.at[o - 1, j, c],
             device_id={"shell": lax.rem(s + o, shells)}, device_id_type=MESH,
         )
 
-    def x_copy(d, j, c, group, row):
-        at = span(row * tile_rows + group * own + c * chunk, chunk)
+    def x_copy(d, j, piece, group, row):
+        c, start, size = piece
+        at = span(row * tile_rows + group * own + start, size)
         return pltpu.make_async_remote_copy(
             src_ref=coupling.at[at], dst_ref=coupling.at[at],
             send_sem=x_send.at[d - 1, j, c], recv_sem=x_recv.at[d - 1, j, c],
             device_id={"row": lax.rem(h + d, chips) * CORES + core}, device_id_type=MESH,
         )
 
-    def f_copy(d, j, c, group, row):
-        at = span(row * tile_rows + group * own + c * chunk, chunk)
+    def f_copy(d, j, piece, group, row):
+        c, start, size = piece
+        at = span(row * tile_rows + group * own + start, size)
         return pltpu.make_async_remote_copy(
             src_ref=coupling.at[at], dst_ref=coupling.at[at],
             send_sem=f_send.at[d, j, c], recv_sem=f_recv.at[d, j, c],
@@ -182,42 +193,51 @@
         if k == 0:
             line = jnp.minimum(col, 1) + jnp.minimum(cols - 1 - col, 1)
             pl.semaphore_wait(barrier, shells - 1 + chips + line)
-        for c in range(pieces):
-            at = span(group * own + c * chunk, chunk)
-            real, imag = combine(c * chunk, chunk)
-            part[at, :width] = real
-            part[at, width:] = imag
-            outgoing[at, :width] = real.astype(bf16)
-            outgoing[at, width:] = imag.astype(bf16)
-            for o in range(1, shells):
-                y_copy(o, (1 + k - o) % shells, c, group).start()
+        for o in range(1, shells):
+            j = (1 + k - o) % shells
+            for piece in parts(j):
+                _, start, size = piece
+                if o == 1:
+                    at = span(group * own + start, size)
+                    real, imag = combine(start, size)
+                    part[at, :width] = real
+                    part[at, width:] = imag
+                    outgoing[at, :width] = real.astype(bf16)
+                    outgoing[at, width:] = imag.astype(bf16)
+                y_copy(o, j, piece, group).start()
 
     def choose(i):
         pivots = pivot_ref[...].reshape(1, -1)
         line = lax.broadcasted_iota(jnp.int32, (128, pivots.shape[1]), 0) + i * 128
         select[i * 128 : (i + 1) * 128, :] = jnp.where(line == pivots, 1.0, 0.0).astype(bf16)
 
-    def take_y(j, c):
+    def forward(d, j, piece, group, row):
+        for bundle in bundles(j):
+            if piece[1] + piece[2] == bundle[1] + bundle[2]:
+                f_copy(d, j, bundle, group, row).start()
+
+    def take_y(j, piece):
+        c, start, size = piece
         group = lax.rem(s + j, shells)
-        at = span(group * own + c * chunk, chunk)
+        at = span(group * own + start, size)
         total = part[at, :]
         for o in range(1, shells):
-            y_copy(o, j, c, group).wait_recv()
+            y_copy(o, j, piece, group).wait_recv()
             total = total + incoming[o - 1, at, :].astype(f32)
-        coupling[span(r * tile_rows + group * own + c * chunk, chunk), :] = total.astype(bf16)
+        coupling[span(r * tile_rows + group * own + start, size), :] = total.astype(bf16)
         if j == 0:
-            owned[c * chunk : (c + 1) * chunk, :] = total
+            owned[start : start + size, :] = total
         for d in range(1, chips):
-            x_copy(d, j, c, group, r).start()
-        f_copy(0, j, c, group, r).start()
-        if j == 0 and (c + 1) * chunk % batch == 0:
+            x_copy(d, j, piece, group, r).start()
+        forward(0, j, piece, group, r)
+        if j == 0:
 
             @pl.when(col == 0)
             def _():
-                base = (c + 1) * chunk - batch
-                if base == 0:
+                if c == 0:
                     inverse_in.wait()
-                panel = owned[base : base + batch, :]
+                batch = size
+                panel = owned[start : start + size, :]
                 high = panel.astype(bf16)
                 low = (panel - high.astype(f32)).astype(bf16)
                 four = jnp.concatenate(
@@ -231,19 +251,19 @@
 
                 m_real = (pick(by_real, 0) - pick(by_imag, 2 * batch)).astype(bf16)
                 m_imag = (pick(by_imag, 0) + pick(by_real, 2 * batch)).astype(bf16)
-                for p in range(halves):
-                    i = base // half + p
+                for p in range(size // half):
+                    i = start // half + p
                     mult[i, 0] = m_real[p * half : (p + 1) * half]
                     mult[i, 1] = m_imag[p * half : (p + 1) * half]
                     if cols > 1:
                         m_copy(i).start()
 
-    def take_x(j, c):
+    def take_x(j, piece):
         group = lax.rem(s + j, shells)
         for d in range(1, chips):
             row = lax.rem(h - d + chips, chips) * CORES + core
-            x_copy(d, j, c, group, row).wait_recv()
-            f_copy(d, j, c, group, row).start()
+            x_copy(d, j, piece, group, row).wait_recv()
+            forward(d, j, piece, group, row)
 
     passes = own // half
 
@@ -257,17 +277,18 @@
                     m_copy(i).wait_recv()
                     m_copy(i).start()
 
-    def take_sibling(d, j, c):
+    def take_sibling(d, j):
         group = lax.rem(s + j, shells)
         row = lax.rem(h - d + chips, chips) * CORES + (CORES - 1 - core)
-        f_copy(d, j, c, group, row).wait_recv()
-
-    steps = [(j, c) for j in range(shells) for c in range(pieces)]
+        for bundle in bundles(j):
+            f_copy(d, j, bundle, group, row).wait_recv()
+
+    steps = [(j, piece) for j in range(shells) for piece in parts(j)]
     lag = 2
     slices = select.shape[0] // 128
     small_in[3].wait()
-    for n, (j, c) in enumerate(steps):
-        take_y(j, c)
+    for n, (j, piece) in enumerate(steps):
+        take_y(j, piece)
         pass_mult(n)
         if n >= lag:
             take_x(*steps[n - lag])
@@ -277,6 +298,9 @@
     for turn in range(len(steps), passes + 2 * cols):
         pass_mult(turn)
 
+    for step in steps[-lag:-1]:
+        take_x(*step)
+
     @pl.when((col == cols - 1) & (col > 0))
     def _():
         for i in range(passes):
@@ -286,18 +310,16 @@
     spread[...] = lax.dot_general(
         factors, select[...], (((1,), (1,)), ((), ())), preferred_element_type=f32
     ).astype(bf16)
-    for j, c in steps:
-        take_sibling(0, j, c)
+    for j in range(shells):
+        take_sibling(0, j)
     near = span(h * CORES * tile_rows, CORES * tile_rows)
     product[...] = jnp.dot(spread[:, near], coupling[near, :], preferred_element_type=f32)
     for j in range(shells):
         if j == shells - 1:
-            for step in steps[-lag:]:
-                take_x(*step)
+            take_x(*steps[-1])
         group = lax.rem(s + j, shells)
         for d in range(1, chips):
-            for c in range(pieces):
-                take_sibling(d, j, c)
+            take_sibling(d, j)
             first_row = lax.rem(h - d + chips, chips) * CORES * tile_rows + group * own
             spots = [span(first_row + i * tile_rows, own) for i in range(CORES)]
             product[...] += jnp.dot(
@@ -309,14 +331,18 @@
     out_ref[0, 0, 0] = owned[:, :width] - real
     out_ref[1, 0, 0] = owned[:, width:] - imag
 
-    for j, c in steps:
+    for j in range(shells):
         group = lax.rem(s + j, shells)
-        for o in range(1, shells):
-            y_copy(o, j, c, group).wait_send()
-        f_copy(0, j, c, group, r).wait_send()
-        for d in range(1, chips):
-            x_copy(d, j, c, group, r).wait_send()
-            f_copy(d, j, c, group, lax.rem(h - d + chips, chips) * CORES + core).wait_send()
+        for piece in parts(j):
+            for o in range(1, shells):
+                k = (j + o - 1) % shells
+                y_copy(o, j, piece, lax.rem(s + 1 + k, shells)).wait_send()
+            for d in range(1, chips):
+                x_copy(d, j, piece, group, r).wait_send()
+        for bundle in bundles(j):
+            f_copy(0, j, bundle, group, r).wait_send()
+            for d in range(1, chips):
+                f_copy(d, j, bundle, group, lax.rem(h - d + chips, chips) * CORES + core).wait_send()
 
     @pl.when(col < cols - 1)
     def _():

time: 23.9 us -> 24.2 us (1.013)
  Pallas kernels: 22.9 us -> 23.2 us
    pallas_call x1, Pallas kernels: 22.9 us -> 23.2 us  [body(): pl.pallas_call(functools.partial(kernel, shells, rows, cols, chunk), out_...]
where the time goes in v2:
time: 24.2 us; the launch traced here: 24 us
  Pallas kernels  23.2 us (96%)
  local copies, waits for them, and re-layouts  0.8 us (3%)
    pallas_call x1, Pallas kernels, body(): pl.pallas_call(functools.partial(kernel, shells, rows, cols, chunk), out_...  23.2 us
    unnamed x1, local copies, waits for them, and re-layouts  0.8 us

profile of v2, /device:TPU:1, one launch (start us, length us, event | category | flops | bytes accessed | tf_op | source)
XLA Modules:
  0.0 24.0 jit_solution(12863913179343391001)
XLA Ops:
  0.0 23.2 %shard_map.73 = f32[2,1,1,128,512]{4,3,2,1,0:T(8,128)S(1)} custom-call(bf16[2,256,768]{2,1,0:T(8,128)(2,1)} %left_hbm.1, bf16[2,768,512]{2,1,0:T(8,128)(2,1)} %right_hbm.1, f32[768]{0:T(1024)} %point_hbm.1, s32[768]{0:T(1024)} %shell_hbm.1, f32[2,12]{1,0:T(2,128)} %bitcast.1, s32[512]{0:T(512)} %pivot_hbm.1, bf16[2,512,512]{2,1,0:T(8,128)(2,1)} %inverse_hbm.1), custom_call_target="tpu_custom_call" | custom-call | flops 1342177280 | bytes 8388608 | tf_op jit(solution)/shard_map/pallas_call | solution.py:387
  23.2 0.8 %copy.9 = f32[2,1,1,128,512]{4,3,2,1,0:T(8,128)} copy(f32[2,1,1,128,512]{4,3,2,1,0:T(8,128)S(1)} %shard_map.73) | data formatting | bytes 1048576

commit v3 on v2

--- a/solution.py
+++ b/solution.py
@@ -26,17 +26,17 @@
     width = right_ref.shape[2]
     tile_rows = left_ref.shape[1]
     own = tile_rows // shells
-    pieces = own // chunk
     half = mult.shape[2]
 
     def places(sizes):
         return [(c, sum(sizes[:c]), size) for c, size in enumerate(sizes)]
 
     def parts(j):
-        return places([chunk] * pieces)
+        short = [chunk // 2] * 2 if j == shells - 1 else [chunk]
+        return places([chunk] * (own // chunk - 1) + short)
 
     def bundles(j):
-        return places([own - 2 * chunk, chunk, chunk] if j == shells - 1 else [own])
+        return places([own - chunk] + [chunk // 2] * 2 if j == shells - 1 else [own])
 
     bf16, f32 = jnp.bfloat16, jnp.float32
 
@@ -269,8 +269,8 @@
 
     def pass_mult(turn):
         for i in range(passes):
-            k, odd = divmod(turn - i, 2)
-            if odd == 0 and 0 < k < cols - 1:
+            k = turn - 1 - i * half // chunk
+            if 0 < k < cols - 1:
 
                 @pl.when(col == k)
                 def _():
@@ -295,7 +295,7 @@
         for i in range(n * slices // len(steps), (n + 1) * slices // len(steps)):
             choose(i)
 
-    for turn in range(len(steps), passes + 2 * cols):
+    for turn in range(len(steps), passes + cols):
         pass_mult(turn)
 
     for step in steps[-lag:-1]:
@@ -357,8 +357,8 @@
     width = right_basis.shape[2]
     own = tile_rows // shells
     chunk = own // 4
-    half = chunk
-    pieces = own // chunk
+    half = chunk // 2
+    pieces = own // chunk + 1
     all_rows = rows * tile_rows
     bf16, f32 = jnp.bfloat16, jnp.float32
     vmem = pl.BlockSpec(memory_space=pltpu.VMEM)

time: 24.2 us -> 24.8 us (1.025)
  Pallas kernels: 23.2 us -> 23.8 us
    pallas_call x1, Pallas kernels: 23.2 us -> 23.8 us  [body(): pl.pallas_call(functools.partial(kernel, shells, rows, cols, chunk), out_...]
where the time goes in v3:
time: 24.8 us; the launch traced here: 24.6 us
  Pallas kernels  23.8 us (96%)
  local copies, waits for them, and re-layouts  0.8 us (3%)
    pallas_call x1, Pallas kernels, body(): pl.pallas_call(functools.partial(kernel, shells, rows, cols, chunk), out_...  23.8 us
    unnamed x1, local copies, waits for them, and re-layouts  0.8 us

profile of v3, /device:TPU:1, one launch (start us, length us, event | category | flops | bytes accessed | tf_op | source)
XLA Modules:
  0.0 24.6 jit_solution(2957350782349460372)
XLA Ops:
  0.0 23.8 %shard_map.73 = f32[2,1,1,128,512]{4,3,2,1,0:T(8,128)S(1)} custom-call(bf16[2,256,768]{2,1,0:T(8,128)(2,1)} %left_hbm.1, bf16[2,768,512]{2,1,0:T(8,128)(2,1)} %right_hbm.1, f32[768]{0:T(1024)} %point_hbm.1, s32[768]{0:T(1024)} %shell_hbm.1, f32[2,12]{1,0:T(2,128)} %bitcast.1, s32[512]{0:T(512)} %pivot_hbm.1, bf16[2,512,512]{2,1,0:T(8,128)(2,1)} %inverse_hbm.1), custom_call_target="tpu_custom_call" | custom-call | flops 1342177280 | bytes 8388608 | tf_op jit(solution)/shard_map/pallas_call | solution.py:387
  23.8 0.8 %copy.9 = f32[2,1,1,128,512]{4,3,2,1,0:T(8,128)} copy(f32[2,1,1,128,512]{4,3,2,1,0:T(8,128)S(1)} %shard_map.73) | data formatting | bytes 1048576

commit v4 on v2

--- a/solution.py
+++ b/solution.py
@@ -33,10 +33,10 @@
         return [(c, sum(sizes[:c]), size) for c, size in enumerate(sizes)]
 
     def parts(j):
-        return places([chunk] * pieces)
+        return places([own - 2 * chunk, chunk, chunk] if j == shells - 1 else [chunk] * pieces)
 
     def bundles(j):
-        return places([own - 2 * chunk, chunk, chunk] if j == shells - 1 else [own])
+        return parts(j) if j == shells - 1 else [(0, 0, own)]
 
     bf16, f32 = jnp.bfloat16, jnp.float32
 
@@ -267,15 +267,22 @@
 
     passes = own // half
 
+    ends = [j * own + start + size for j in range(shells) for _, start, size in parts(j)]
+
+    def turn_of(i, k):
+        rows_by_then = (2 * i + 4 + 3 * k) * half // 2
+        late = [n for n in range(len(ends) - 1) if ends[n + 1] >= rows_by_then]
+        return late[0] if late else len(ends)
+
     def pass_mult(turn):
-        for i in range(passes):
-            k, odd = divmod(turn - i, 2)
-            if odd == 0 and 0 < k < cols - 1:
-
-                @pl.when(col == k)
-                def _():
-                    m_copy(i).wait_recv()
-                    m_copy(i).start()
+        for k in range(1, cols - 1):
+            for i in range(passes):
+                if turn == turn_of(i, k):
+
+                    @pl.when(col == k)
+                    def _():
+                        m_copy(i).wait_recv()
+                        m_copy(i).start()
 
     def take_sibling(d, j):
         group = lax.rem(s + j, shells)
@@ -295,8 +302,7 @@
         for i in range(n * slices // len(steps), (n + 1) * slices // len(steps)):
             choose(i)
 
-    for turn in range(len(steps), passes + 2 * cols):
-        pass_mult(turn)
+    pass_mult(len(steps))
 
     for step in steps[-lag:-1]:
         take_x(*step)

time: 24.2 us -> 24.9 us (1.029)
  Pallas kernels: 23.2 us -> 23.9 us
    pallas_call x1, Pallas kernels: 23.2 us -> 23.9 us  [body(): pl.pallas_call(functools.partial(kernel, shells, rows, cols, chunk), out_...]
where the time goes in v4:
time: 24.9 us; the launch traced here: 24.7 us
  Pallas kernels  23.9 us (96%)
  local copies, waits for them, and re-layouts  0.8 us (3%)
    pallas_call x1, Pallas kernels, body(): pl.pallas_call(functools.partial(kernel, shells, rows, cols, chunk), out_...  23.9 us
    unnamed x1, local copies, waits for them, and re-layouts  0.8 us

profile of v4, /device:TPU:1, one launch (start us, length us, event | category | flops | bytes accessed | tf_op | source)
XLA Modules:
  0.0 24.7 jit_solution(13677518451712336002)
XLA Ops:
  0.0 23.9 %shard_map.73 = f32[2,1,1,128,512]{4,3,2,1,0:T(8,128)S(1)} custom-call(bf16[2,256,768]{2,1,0:T(8,128)(2,1)} %left_hbm.1, bf16[2,768,512]{2,1,0:T(8,128)(2,1)} %right_hbm.1, f32[768]{0:T(1024)} %point_hbm.1, s32[768]{0:T(1024)} %shell_hbm.1, f32[2,12]{1,0:T(2,128)} %bitcast.1, s32[512]{0:T(512)} %pivot_hbm.1, bf16[2,512,512]{2,1,0:T(8,128)(2,1)} %inverse_hbm.1), custom_call_target="tpu_custom_call" | custom-call | flops 1342177280 | bytes 8388608 | tf_op jit(solution)/shard_map/pallas_call | solution.py:393
  23.9 0.8 %copy.9 = f32[2,1,1,128,512]{4,3,2,1,0:T(8,128)} copy(f32[2,1,1,128,512]{4,3,2,1,0:T(8,128)S(1)} %shard_map.73) | data formatting | bytes 1048576
